TPU v7x, 512 devices: a whole 4x4x16 slice. The times are simulated.
512 devices in a mesh: ens: 16 (over y_lo, x, core), lat: 16 (over z), dp: 2 (over y_hi).
Axes of the slice: x: 4, y: 4 (y_hi: 2, y_lo: 2; y = y_hi * 2 + y_lo), z: 16, core: 2. Of those that a mesh axis runs over, the one named last changes fastest.
Arguments:
- features: bfloat16 [2, 16, 256, 32, 512], P('dp', 'ens', None, 'lat'), may hold values from -6 to 6
- members_out: bfloat16 [2, 16, 72, 32, 512], P('dp', 'ens', None, 'lat'), may hold values from -6 to 6
- observed: float32 [2, 72, 32, 512], P('dp', None, 'lat'), may hold values from -6 to 6
- conv_weight: bfloat16 [9, 72, 256], replicated, may hold values from -0.125 to 0.125
- lat_weight: float32 [32], P('lat'), may hold values from 0.2 to 1
- var_weight: float32 [72], replicated, may hold values from 0.3 to 3
- land_mask: int32 [32, 512], P('lat'), may hold values 0 or 1
Outputs:
- feature_grads: bfloat16 [2, 16, 256, 32, 512], P('dp', 'ens', None, 'lat')
- grad_weight: float32 [9, 72, 256], replicated
All inputs are finite; a program needn't handle non-finite values. No bound on the sum of `land_mask` on one device may be relied on, other than what follows from the above.
Results may differ from a plain program's by a relative error of at most 0.0049.
Values may be sent and summed in bfloat16 or wider, within the bound.
A program may use at most 64 MiB of HBM per device.

v0:
```python
import math

import jax
import jax.numpy as jnp
from jax import lax
from jax.sharding import PartitionSpec as P


def padded_2(value, sides, width):
    for axis, dim in sides:
        count, length = (lax.axis_size(axis), value.shape[dim])
        up = [(i, (i + 1) % count) for i in range(count - 1)]
        down = [(j, i) for i, j in up]
        last = lax.slice_in_dim(value, length - width, length, axis=dim)
        leading = lax.slice_in_dim(value, 0, width, axis=dim)
        before = lax.ppermute(last, axis, up)
        after = lax.ppermute(leading, axis, down)
        value = jnp.concatenate([before, value, after], axis=dim)
    return value


def local(features, members_out, observed, conv_weight, lat_weight, var_weight, land_mask):
    channels = features.shape[2]
    lat_rows = features.shape[3]
    lon_cells = features.shape[4]
    variables = members_out.shape[2]
    members = lax.axis_size("ens")
    cell_weight = (
        lat_weight[None, :, None]
        * var_weight[:, None, None]
        * (1.0 + land_mask.astype(jnp.float32))[None]
    )
    own_field = members_out[0, 0].astype(jnp.float32)
    pair_sums = jnp.sum(
        jnp.sign(
            own_field[None]
            - lax.all_gather(members_out, "ens", axis=1, tiled=True)[0].astype(jnp.float32)
        ),
        axis=0,
    )
    out_grads = (
        cell_weight * (jnp.sign(own_field - observed[0]) - pair_sums / (members - 1))
    ).astype(jnp.bfloat16)
    padded = padded_2(out_grads, (("lat", 1),), 1)
    padded = jnp.pad(padded, ((0, 0), (0, 0), (1, 1)))
    slices = []
    for row_shift in (-1, 0, 1):
        for col_shift in (-1, 0, 1):
            slices.append(
                padded[
                    :,
                    1 - row_shift : 1 - row_shift + lat_rows,
                    1 - col_shift : 1 - col_shift + lon_cells,
                ]
            )
    tap_rows = jnp.stack(slices).reshape(9 * variables, lat_rows * lon_cells)
    flat_weight = conv_weight.reshape(9 * variables, channels)
    feature_grad = jnp.einsum(
        "kc,kn->cn", flat_weight, tap_rows, preferred_element_type=jnp.float32
    )
    feature_grad = feature_grad.astype(jnp.bfloat16).reshape(1, 1, channels, lat_rows, lon_cells)
    flat_feats = features[0, 0].reshape(channels, lat_rows * lon_cells)
    weight_grad = jnp.einsum("kn,cn->kc", tap_rows, flat_feats, preferred_element_type=jnp.float32)
    term_count = lax.axis_size("dp") * members * lax.axis_size("lat") * lat_rows * lon_cells
    factor = 1.0 / math.sqrt(term_count)
    summed = lax.psum(weight_grad, ("ens", "lat", "dp"))
    grad_weight = (summed * factor).reshape(9, variables, channels)
    return (feature_grad, grad_weight)


def solution(mesh):
    return jax.shard_map(
        local,
        mesh=mesh,
        in_specs=(
            P("dp", "ens", None, "lat", None),
            P("dp", "ens", None, "lat", None),
            P("dp", None, "lat", None),
            P(),
            P("lat"),
            P(),
            P("lat", None),
        ),
        out_specs=(P("dp", "ens", None, "lat", None), P()),
        check_vma=False,
    )
```

profile of v0, /device:TPU:1, one launch (start us, length us, event | category | flops | bytes accessed | tf_op | source)
XLA Modules:
  0.0 547.4 jit_solution(16325097610128155280)
XLA Ops:
  7.2 0.0 copy-start
  7.2 0.0 all-gather.2.cloned.1.call-start
  7.2 1.6 copy.20
  8.9 0.0 all-gather.2.cloned.1.call-update
  8.9 0.0 all-reduce.3.cloned.1.call-start
  8.9 0.7 broadcast_multiply_fusion.1
  9.7 0.7 convert_add_fusion
  10.4 0.9 convert_bitcast_fusion.1
  11.3 0.0 copy-start.1
  11.3 0.0 copy-start.2
  11.3 47.2 %all-gather.2.cloned.1.call-done = bf16[1,16,72,2,512]{4,2,3,0,1:T(8,128)(2,1)} async-done(((bf16[1,1,72,2,512]{4,2,3,0,1:T(8,128)(2,1)}), bf16[1,16,72,2,512]{4,2,3,0,1:T(8,128)(2,1)}) %all-gather.2.cloned.1.call-update) | async-done | bytes 2359312 | tf_op jit(solution)/shard_map/all_gather | solution.py:37
  58.5 3.2 fusion.1
  61.7 0.0 copy-start.3
  61.8 0.1 fusion.16
  61.9 3.1 collective-permute-start
  65.0 1.3 collective-permute-start.1
  66.3 0.1 copy.25
  66.4 0.0 collective-permute-done
  66.4 3.7 collective-permute-done.1
  70.1 0.2 fusion.7
  70.3 0.1 fusion.27
  70.5 0.1 fusion.23
  70.6 0.1 fusion.17
  70.8 0.1 fusion.21
  70.9 1.1 copy.22
  72.0 0.3 copy.24
  72.3 1.4 fusion.29
  73.8 0.0 all-reduce.3.cloned.1.call-update
  73.8 0.7 convolution_convert_fusion
  74.5 1.2 copy.23
  75.7 462.9 %all-reduce.3.cloned.1.call-done = f32[648,256]{1,0:T(8,128)} async-done(((f32[648,256]{1,0:T(8,128)}), f32[648,256]{1,0:T(8,128)}) %all-reduce.3.cloned.1.call-update) | async-done | bytes 663568 | tf_op jit(solution)/shard_map/psum | solution.py:66
  538.6 2.0 broadcast_multiply_fusion
  (10 shorter events, 0.1 us)
Async XLA Ops:
  7.2 66.6 %copy-start = (bf16[9,72,256]{2,1,0:T(8,128)(2,1)S(1)}, bf16[9,72,256]{2,1,0:T(8,128)(2,1)}, u32[]{:S(2)}) copy-start(bf16[9,72,256]{2,1,0:T(8,128)(2,1)} %param.10) | copy-start | bytes 995332
  7.2 51.3 %all-gather.2.cloned.1.call-start = ((), (), s32[]{:S(2)}) async-start(), calls=%async_computation | async-start | bytes 2506752 | tf_op jit(solution)/shard_map/all_gather | solution.py:37
  8.9 529.7 %all-reduce.3.cloned.1.call-start = ((), (), s32[]{:S(2)}) async-start(), calls=%async_computation.1 | async-start | bytes 1327104 | tf_op jit(solution)/shard_map/psum | solution.py:66
  11.3 50.4 %copy-start.1 = (bf16[1,1,72,2,512]{4,3,2,1,0:T(2,128)(2,1)S(1)}, bf16[1,1,72,2,512]{4,3,2,1,0:T(2,128)(2,1)}, u32[]{:S(2)}) copy-start(bf16[1,1,72,2,512]{4,3,2,1,0:T(2,128)(2,1)} %param.8) | copy-start | bytes 442372
  11.3 50.4 %copy-start.2 = (f32[1,72,2,512]{3,2,1,0:T(2,128)S(1)}, f32[1,72,2,512]{3,2,1,0:T(2,128)}, u32[]{:S(2)}) copy-start(f32[1,72,2,512]{3,2,1,0:T(2,128)} %param.9) | copy-start | bytes 884740
  61.7 4.6 copy-start.3
  61.9 4.5 collective-permute-start
  65.0 5.1 collective-permute-start.1
Sparse Core Ops, SparseCore 0:
  10.7 47.7 all-gather.1
  73.9 464.6 all-reduce.2
where the time goes:
time: 548 us; the launch traced here: 547 us
  waiting for transfers between devices  514 us (94%)
  between operations  14.3 us (3%)
  other arithmetic  8.11 us (1%)
    psum x1, waiting for transfers between devices, local(): summed = lax.psum(weight_grad, ('ens', 'lat', 'dp'))  463 us
    all_gather x1, waiting for transfers between devices, local(): lax.all_gather(members_out, 'ens', axis=1, tiled=True)[0]  47.2 us
  transfers between devices with their start and end apart: 4, of which 3 were waited for; matrix products, arithmetic and copies ran while one was open for 1% of the time, Pallas kernels for 0%

commit v1 on v0

v1 whole, which is shorter than its diff:
```python
import functools
import math

import jax
import jax.numpy as jnp
from jax import lax
from jax.experimental import pallas as pl
from jax.experimental.pallas import tpu as pltpu
from jax.sharding import PartitionSpec as P

MESH = pl.DeviceIdType.MESH
BF16 = jnp.bfloat16
F32 = jnp.float32

MEMBERS = 16
BANDS = 16
VARS = 72
PAD_VARS = 80
LONS = 512
CHANS = 256
OWNERS = 12
CHUNK = 48
RAW = VARS * 8
TAPS = 9 * PAD_VARS
CHIPS = 16
PIECE = 48
ROWS = CHIPS * PIECE


def kernel(
    members_ref, obs_ref, feats_ref, weight_ref, lat_ref, var_ref, land_ref,
    fg_ref, gw_ref,
    mbuf, obuf, gbuf, gf, obs, feats, weight, stack, fgbuf, wg, wgin, pieces, rs, za, zb,
    exch_send, exch_recv, back_send, back_recv, halo_send, halo_recv, core_send, core_recv,
    rs_send, rs_recv, za_send, za_recv, zb_send, zb_recv, ag_send, ag_recv, fwd_send, fwd_recv,
    load_sem, store_sem,
):
    ens = lax.axis_index("ens")
    lat = lax.axis_index("lat")
    dp = lax.axis_index("dp")
    core = lax.rem(ens, 2)
    chip = dp * 8 + ens // 2
    up = lax.rem(lat + 1, BANDS)
    down = lax.rem(lat + BANDS - 1, BANDS)
    zlo = lax.rem(lat, 4)
    zhi = lat // 4

    def at(e, l, d):
        return (e, l, d)

    barrier = pltpu.get_barrier_semaphore()

    def greet(e, l, d):
        pl.semaphore_signal(barrier, inc=1, device_id=at(e, l, d), device_id_type=MESH)

    def greet_ens(k, c):
        greet(lax.rem(ens + k, MEMBERS), lat, dp)
        return c

    lax.fori_loop(1, MEMBERS, greet_ens, 0)

    def greet_dp(k, c):
        greet(2 * k + core, lat, 1 - dp)
        return c

    lax.fori_loop(0, 8, greet_dp, 0)
    greet(ens, up, dp)
    greet(ens, down, dp)

    def greet_z(k, c):
        greet(ens, zhi * 4 + lax.rem(zlo + k, 4), dp)
        greet(ens, lax.rem(lat + 4 * k, BANDS), dp)
        return c

    lax.fori_loop(1, 4, greet_z, 0)

    load_obs = pltpu.make_async_copy(obs_ref.at[pl.ds(jnp.minimum(ens, OWNERS - 1) * CHUNK, CHUNK)], obs, load_sem.at[0])
    load_obs.start()
    load_feats = pltpu.make_async_copy(feats_ref, feats, load_sem.at[1])
    load_feats.start()
    load_weight = pltpu.make_async_copy(weight_ref, weight, load_sem.at[2])
    load_weight.start()

    pl.semaphore_wait(barrier, 15 + 8 + 2 + 6)

    def send_chunk(k, c):
        owner = lax.rem(ens + k, MEMBERS)

        @pl.when(owner < OWNERS)
        def _():
            pltpu.make_async_remote_copy(
                src_ref=members_ref.at[pl.ds(owner * CHUNK, CHUNK)],
                dst_ref=mbuf.at[ens],
                send_sem=exch_send, recv_sem=exch_recv,
                device_id=at(owner, lat, dp), device_id_type=MESH,
            ).start()
        return c

    lax.fori_loop(1, MEMBERS, send_chunk, 0)
    owned = ens < OWNERS

    @pl.when(owned)
    def _():
        mine = pltpu.make_async_copy(members_ref.at[pl.ds(ens * CHUNK, CHUNK)], mbuf.at[ens], exch_recv)
        mine.start()
    load_obs.wait()

    @pl.when(owned)
    def _():
        pltpu.make_async_copy(mbuf, mbuf, exch_recv).wait()

        one = jnp.ones((16, 128), F32)
        zero = jnp.zeros((16, 128), F32)
        row = lax.broadcasted_iota(jnp.int32, (8, 128), 0)
        lat_rows = jnp.where(lax.rem(row, 2) == 0, lat_ref[0], lat_ref[1])
        land_rows = 1.0 + land_ref[...].astype(F32)

        def tile(u, c):
            rows = pl.ds(pl.multiple_of(u * 16, 16), 16)
            vals = [mbuf[m, rows, :].astype(F32) for m in range(MEMBERS)]
            sums = [None] * MEMBERS
            for i in range(MEMBERS):
                for j in range(i + 1, MEMBERS):
                    s = jnp.where(vals[i] > vals[j], one, jnp.where(vals[i] < vals[j], -one, zero))
                    sums[i] = s if sums[i] is None else sums[i] + s
                    sums[j] = -s if sums[j] is None else sums[j] - s
            seen = obs[rows, :]
            v0 = ens * 6 + u * 2
            cell = jnp.concatenate(
                [(lat_rows * var_ref[v0]) * land_rows, (lat_rows * var_ref[v0 + 1]) * land_rows], axis=0
            )
            for m in range(MEMBERS):
                s = jnp.where(vals[m] > seen, one, jnp.where(vals[m] < seen, -one, zero))
                obuf[m, rows, :] = (cell * (s - sums[m] / (MEMBERS - 1))).astype(BF16)
            return c

        lax.fori_loop(0, CHUNK // 16, tile, 0)

        def send_back(k, c):
            m = lax.rem(ens + k, MEMBERS)
            pltpu.make_async_remote_copy(
                src_ref=obuf.at[m],
                dst_ref=gbuf.at[pl.ds(ens * CHUNK, CHUNK)],
                send_sem=back_send, recv_sem=back_recv,
                device_id=at(m, lat, dp), device_id_type=MESH,
            ).start()
            return c

        lax.fori_loop(1, MEMBERS, send_back, 0)
        pltpu.make_async_copy(obuf.at[ens], gbuf.at[pl.ds(ens * CHUNK, CHUNK)], back_recv).start()

    pltpu.make_async_copy(gbuf, gbuf, back_recv).wait()

    col = lax.broadcasted_iota(jnp.int32, (PAD_VARS, LONS), 1)

    def put(slot, x):
        stack[slot, 1] = x.astype(BF16)
        stack[slot, 0] = jnp.where(col == 0, 0.0, pltpu.roll(x, 1, 1)).astype(BF16)
        stack[slot, 2] = jnp.where(col == LONS - 1, 0.0, pltpu.roll(x, LONS - 1, 1)).astype(BF16)

    gf[...] = gbuf[...].astype(F32)
    rows = []
    for r in range(2):
        x = jnp.concatenate([gf[pl.ds(2 * l + r, VARS, stride=8), :] for l in range(4)], axis=1)
        rows.append(jnp.concatenate([x, jnp.zeros((PAD_VARS - VARS, LONS), F32)], axis=0))
        stack[r + 1, 1] = rows[r].astype(BF16)
    halo = []
    for r in range(2):
        halo.append(pltpu.make_async_remote_copy(
            src_ref=stack.at[r + 1, 1], dst_ref=stack.at[3 - 3 * r, 1],
            send_sem=halo_send.at[r], recv_sem=halo_recv.at[r],
            device_id=at(ens, down if r == 0 else up, dp), device_id_type=MESH,
        ))
        halo[r].start()
    for r in range(2):
        stack[r + 1, 0] = jnp.where(col == 0, 0.0, pltpu.roll(rows[r], 1, 1)).astype(BF16)
        stack[r + 1, 2] = jnp.where(col == LONS - 1, 0.0, pltpu.roll(rows[r], LONS - 1, 1)).astype(BF16)
    load_feats.wait()
    load_weight.wait()
    for r in range(2):
        halo[r].wait()
    put(3, jnp.where(lat == BANDS - 1, 0.0, stack[3, 1].astype(F32)))
    put(0, jnp.where(lat == 0, 0.0, stack[0, 1].astype(F32)))

    def half(h):
        total = None
        for r in range(2):
            taps = stack[pl.ds(r, 3)].reshape(TAPS, LONS)
            part = lax.dot_general(
                taps, feats[r, pl.ds(pl.multiple_of(h * 128, 128), 128), :], (((1,), (1,)), ((), ())),
                preferred_element_type=F32,
            )
            total = part if total is None else total + part
        return total

    wg[0] = half(1 - core)
    to_core = pltpu.make_async_remote_copy(
        src_ref=wg.at[0], dst_ref=wgin, send_sem=core_send, recv_sem=core_recv,
        device_id=at(ens + 1 - 2 * core, lat, dp), device_id_type=MESH,
    )
    to_core.start()
    wg[1] = half(core)
    to_core.wait()
    summed = wg[1] + wgin[...]
    pieces[pl.ds(0, TAPS), :] = summed.astype(BF16)
    pieces[pl.ds(TAPS, ROWS - TAPS), :] = jnp.zeros((ROWS - TAPS, 128), BF16)

    def send_piece(k, c):
        q = lax.rem(chip + k, CHIPS)
        pltpu.make_async_remote_copy(
            src_ref=pieces.at[pl.ds(q * PIECE, PIECE)], dst_ref=rs.at[chip],
            send_sem=rs_send, recv_sem=rs_recv,
            device_id=at(lax.rem(q, 8) * 2 + core, lat, q // 8), device_id_type=MESH,
        ).start()
        return c

    lax.fori_loop(1, CHIPS, send_piece, 0)
    pltpu.make_async_copy(pieces.at[pl.ds(chip * PIECE, PIECE)], rs.at[chip], rs_recv).start()

    for r in range(2):
        taps = stack[pl.ds(r, 3)].reshape(TAPS, LONS)
        fgbuf[r] = jnp.dot(weight[...], taps, preferred_element_type=F32).astype(BF16)
    store_fg = pltpu.make_async_copy(fgbuf, fg_ref, store_sem)
    store_fg.start()

    pltpu.make_async_copy(rs, rs, rs_recv).wait()
    piece = rs[0].astype(F32)
    for q in range(1, CHIPS):
        piece = piece + rs[q].astype(F32)

    za[zlo] = piece.astype(BF16)
    for k in range(1, 4):
        pltpu.make_async_remote_copy(
            src_ref=za.at[zlo], dst_ref=za.at[zlo], send_sem=za_send, recv_sem=za_recv,
            device_id=at(ens, zhi * 4 + lax.rem(zlo + k, 4), dp), device_id_type=MESH,
        ).start()
    pltpu.make_async_copy(za.at[pl.ds(0, 3)], za.at[pl.ds(0, 3)], za_recv).wait()
    piece = (za[0].astype(F32) + za[1].astype(F32)) + (za[2].astype(F32) + za[3].astype(F32))
    zb[zhi] = piece.astype(BF16)
    for k in range(1, 4):
        pltpu.make_async_remote_copy(
            src_ref=zb.at[zhi], dst_ref=zb.at[zhi], send_sem=zb_send, recv_sem=zb_recv,
            device_id=at(ens, lax.rem(lat + 4 * k, BANDS), dp), device_id_type=MESH,
        ).start()
    pltpu.make_async_copy(zb.at[pl.ds(0, 3)], zb.at[pl.ds(0, 3)], zb_recv).wait()
    piece = (zb[0].astype(F32) + zb[1].astype(F32)) + (zb[2].astype(F32) + zb[3].astype(F32))
    za[4] = piece.astype(BF16)

    def send_sum(k, c):
        q = lax.rem(chip + k, CHIPS)
        pltpu.make_async_remote_copy(
            src_ref=za.at[4], dst_ref=gw_ref.at[core, chip],
            send_sem=ag_send, recv_sem=ag_recv,
            device_id=at(lax.rem(q, 8) * 2 + core, lat, q // 8), device_id_type=MESH,
        ).start()
        return c

    lax.fori_loop(1, CHIPS, send_sum, 0)
    pltpu.make_async_copy(za.at[4], gw_ref.at[core, chip], ag_recv).start()
    pltpu.make_async_copy(rs, rs, ag_recv).wait()
    forward = pltpu.make_async_remote_copy(
        src_ref=gw_ref.at[core], dst_ref=gw_ref.at[core], send_sem=fwd_send, recv_sem=fwd_recv,
        device_id=at(ens + 1 - 2 * core, lat, dp), device_id_type=MESH,
    )
    forward.start()

    @pl.when(owned)
    def _():
        pltpu.make_async_copy(mbuf.at[pl.ds(0, OWNERS - 1)], mbuf.at[pl.ds(0, OWNERS - 1)], exch_send).wait()
        pltpu.make_async_copy(obuf.at[pl.ds(0, MEMBERS - 1)], obuf.at[pl.ds(0, MEMBERS - 1)], back_send).wait()

    @pl.when(jnp.logical_not(owned))
    def _():
        pltpu.make_async_copy(mbuf.at[pl.ds(0, OWNERS)], mbuf.at[pl.ds(0, OWNERS)], exch_send).wait()

    pltpu.make_async_copy(rs.at[pl.ds(0, CHIPS - 1)], rs.at[pl.ds(0, CHIPS - 1)], rs_send).wait()
    pltpu.make_async_copy(za.at[pl.ds(0, 3)], za.at[pl.ds(0, 3)], za_send).wait()
    pltpu.make_async_copy(zb.at[pl.ds(0, 3)], zb.at[pl.ds(0, 3)], zb_send).wait()
    pltpu.make_async_copy(rs.at[pl.ds(0, CHIPS - 1)], rs.at[pl.ds(0, CHIPS - 1)], ag_send).wait()
    store_fg.wait()
    forward.wait()


def raw_rows(x):
    lead = x.shape[0]
    return x.reshape(lead, 2, 4, 128).transpose(0, 2, 1, 3).reshape(lead * 8, 128)


def local(features, members_out, observed, conv_weight, lat_weight, var_weight, land_mask):
    members = raw_rows(members_out[0, 0])
    obs = raw_rows(observed[0])
    land = raw_rows(land_mask[None])
    feats = features[0, 0].transpose(1, 0, 2)
    weight = jnp.pad(conv_weight[::-1], ((0, 0), (0, PAD_VARS - VARS), (0, 0))).reshape(TAPS, CHANS).T
    any_spec = pl.BlockSpec(memory_space=pl.ANY)
    vmem_spec = pl.BlockSpec(memory_space=pltpu.VMEM)
    smem_spec = pl.BlockSpec(memory_space=pltpu.SMEM)
    dma = pltpu.SemaphoreType.DMA
    fg, gw = pl.pallas_call(
        kernel,
        out_shape=(
            jax.ShapeDtypeStruct((2, CHANS, LONS), BF16),
            jax.ShapeDtypeStruct((2, CHIPS, PIECE, 128), BF16),
        ),
        in_specs=[any_spec, any_spec, any_spec, any_spec, smem_spec, smem_spec, vmem_spec],
        out_specs=(any_spec, any_spec),
        scratch_shapes=[
            pltpu.VMEM((MEMBERS, CHUNK, 128), BF16),
            pltpu.VMEM((MEMBERS, CHUNK, 128), BF16),
            pltpu.VMEM((RAW, 128), BF16),
            pltpu.VMEM((RAW, 128), F32),
            pltpu.VMEM((CHUNK, 128), F32),
            pltpu.VMEM((2, CHANS, LONS), BF16),
            pltpu.VMEM((CHANS, TAPS), BF16),
            pltpu.VMEM((4, 3, PAD_VARS, LONS), BF16),
            pltpu.VMEM((2, CHANS, LONS), BF16),
            pltpu.VMEM((2, TAPS, 128), F32),
            pltpu.VMEM((TAPS, 128), F32),
            pltpu.VMEM((ROWS, 128), BF16),
            pltpu.VMEM((CHIPS, PIECE, 128), BF16),
            pltpu.VMEM((5, PIECE, 128), BF16),
            pltpu.VMEM((4, PIECE, 128), BF16),
            dma, dma, dma, dma, dma((2,)), dma((2,)), dma, dma,
            dma, dma, dma, dma, dma, dma, dma, dma, dma, dma,
            dma((3,)), dma,
        ],
        compiler_params=pltpu.CompilerParams(
            collective_id=0, has_side_effects=True, vmem_limit_bytes=32 * 1024 * 1024
        ),
        name="crps_backward",
    )(members, obs, feats, weight, lat_weight, var_weight, land)
    feature_grad = fg.transpose(1, 0, 2)[None, None]
    factor = 1.0 / math.sqrt(2 * MEMBERS * 32 * LONS)
    flat = gw.reshape(2, ROWS, 128)[:, :TAPS].reshape(2, 9, PAD_VARS, 128)[:, ::-1, :VARS]
    grad_weight = flat.transpose(1, 2, 0, 3).reshape(9, VARS, CHANS).astype(F32) * factor
    return (feature_grad, grad_weight)


def solution(mesh):
    return jax.shard_map(
        local,
        mesh=mesh,
        in_specs=(
            P("dp", "ens", None, "lat", None),
            P("dp", "ens", None, "lat", None),
            P("dp", None, "lat", None),
            P(),
            P("lat"),
            P(),
            P("lat", None),
        ),
        out_specs=(P("dp", "ens", None, "lat", None), P()),
        check_vma=False,
    )
```

time: 548 us -> 63.2 us (0.12)
  waiting for transfers between devices: 514 us -> 0 us
  Pallas kernels: 0 us -> 55.9 us
  between operations: 14.3 us -> 0.71 us
  other arithmetic: 8.11 us -> 0.34 us
    psum x1 -> x0, waiting for transfers between devices: 463 us -> none  [local(): summed = lax.psum(weight_grad, ('ens', 'lat', 'dp'))]
    pallas_call x0 -> x1, Pallas kernels: none -> 55.9 us  [local(): pl.pallas_call(kernel, out_shape=(jax.ShapeDtypeStruct((2, CHANS, LONS),...]
    all_gather x1 -> x0, waiting for transfers between devices: 47.2 us -> none  [local(): lax.all_gather(members_out, 'ens', axis=1, tiled=True)[0]]
  transfers between devices with their start and end apart: 4 -> 0, of which waited for: 3 -> 0; matrix products, arithmetic and copies ran while one was open for 1% -> 0% of each run, Pallas kernels for 0% -> 0%
where the time goes in v1:
time: 63.2 us; the launch traced here: 63 us
  Pallas kernels  55.9 us (88%)
  local copies, waits for them, and re-layouts  6.05 us (10%)
  between operations  0.71 us (1%)
    pallas_call x1, Pallas kernels, local(): pl.pallas_call(kernel, out_shape=(jax.ShapeDtypeStruct((2, CHANS, LONS),...  55.9 us
    unnamed x15, local copies, waits for them, and re-layouts  3.43 us
    mul x1, local copies, waits for them, and re-layouts, local(): flat.transpose(1, 2, 0, 3).reshape(9, VARS, CHANS).astype(F32) * factor  1.37 us

profile of v1, /device:TPU:1, one launch (start us, length us, event | category | flops | bytes accessed | tf_op | source)
XLA Modules:
  0.0 63.0 jit_solution(1216845455477220160)
XLA Ops:
  0.6 1.0 %rev.6 = bf16[9,72,256]{2,1,0:T(8,128)(2,1)S(1)} reverse(bf16[9,72,256]{2,1,0:T(8,128)(2,1)} %param.10), dimensions={0} | reverse | bytes 663552 | tf_op jit(solution)/shard_map/rev | solution.py:294
  1.7 0.0 copy-start.5
  1.7 0.2 copy.19
  1.9 0.9 %copy-done.5 = bf16[1,1,256,2,512]{4,3,2,1,0:T(2,128)(2,1)S(1)} copy-done((bf16[1,1,256,2,512]{4,3,2,1,0:T(2,128)(2,1)S(1)}, bf16[1,1,256,2,512]{4,3,2,1,0:T(2,128)(2,1)}, u32[]{:S(2)}) %copy-start.5) | copy-done | bytes 524312
  2.7 0.0 copy-start
  2.7 0.0 copy-start.1
  2.7 0.0 copy-start.2
  2.7 0.1 copy.25
  2.8 0.0 copy-start.3
  2.8 0.0 copy-start.4
  2.8 0.9 %copy-done = f32[1,72,2,512]{3,2,1,0:T(2,128)S(1)} copy-done((f32[1,72,2,512]{3,2,1,0:T(2,128)S(1)}, f32[1,72,2,512]{3,2,1,0:T(2,128)}, u32[]{:S(2)}) %copy-start) | copy-done | bytes 294936
  3.7 0.0 copy-done.1
  3.7 0.0 copy-done.2
  3.7 0.0 copy-done.3
  3.7 0.0 copy-done.4
  3.7 55.9 %crps_backward.1 = (bf16[2,256,512]{2,1,0:T(8,128)(2,1)S(1)}, bf16[2,16,48,128]{3,2,1,0:T(8,128)(2,1)S(1)}) custom-call(bf16[576,128]{1,0:T(8,128)(2,1)S(1)} %bitcast.34, f32[576,128]{1,0:T(8,128)S(1)} %bitcast.33, bf16[2,256,512]{2,1,0:T(8,128)(2,1)S(1)} %bitcast.29, bf16[256,720]{1,0:T(8,128)(2,1)S(1)} %bitcast.30, f32[2]{0:T(128)S(1)} %copy-done.3, ...), custom_call_target="tpu_custom_call" | custom-call | tf_op jit(solution)/shard_map/crps_backward/pallas_call | solution.py:299
  59.6 1.3 %copy.22 = bf16[1,1,256,2,512]{4,3,2,1,0:T(2,128)(2,1)} copy(bf16[1,1,256,2,512]{4,2,3,1,0:T(8,128)(2,1)S(1)} %bitcast.31) | data formatting | bytes 1048576
  61.0 0.3 copy.23
  61.3 0.3 multiply_bitcast_fusion
  61.6 1.4 %mul.15 = f32[9,72,256]{2,1,0:T(8,128)} reshape(f32[9,72,2,128]{3,2,1,0:T(2,128)S(1)} %multiply_bitcast_fusion) | data formatting | bytes 1327104 | tf_op jit(solution)/shard_map/mul | solution.py:335
  (3 shorter events, 0.1 us)
Async XLA Ops:
  1.7 1.0 %copy-start.5 = (bf16[1,1,256,2,512]{4,3,2,1,0:T(2,128)(2,1)S(1)}, bf16[1,1,256,2,512]{4,3,2,1,0:T(2,128)(2,1)}, u32[]{:S(2)}) copy-start(bf16[1,1,256,2,512]{4,3,2,1,0:T(2,128)(2,1)} %param.7) | copy-start | bytes 1572868
  2.7 1.0 %copy-start = (f32[1,72,2,512]{3,2,1,0:T(2,128)S(1)}, f32[1,72,2,512]{3,2,1,0:T(2,128)}, u32[]{:S(2)}) copy-start(f32[1,72,2,512]{3,2,1,0:T(2,128)} %param.9) | copy-start | bytes 884740
  2.7 1.0 %copy-start.1 = (bf16[1,1,72,2,512]{4,3,2,1,0:T(2,128)(2,1)S(1)}, bf16[1,1,72,2,512]{4,3,2,1,0:T(2,128)(2,1)}, u32[]{:S(2)}) copy-start(bf16[1,1,72,2,512]{4,3,2,1,0:T(2,128)(2,1)} %param.8) | copy-start | bytes 442372
  2.7 1.0 %copy-start.2 = (s32[2,512]{1,0:T(2,128)S(1)}, s32[2,512]{1,0:T(2,128)}, u32[]{:S(2)}) copy-start(s32[2,512]{1,0:T(2,128)} %param.13) | copy-start | bytes 12292
  2.8 0.9 %copy-start.3 = (f32[2]{0:T(128)S(1)}, f32[2]{0:T(128)}, u32[]{:S(2)}) copy-start(f32[2]{0:T(128)} %lat_ref.1) | copy-start | bytes 28
  2.8 0.9 %copy-start.4 = (f32[72]{0:T(128)S(1)}, f32[72]{0:T(128)}, u32[]{:S(2)}) copy-start(f32[72]{0:T(128)} %var_ref.1) | copy-start | bytes 868

commit v2 on v0

v2 whole, which is shorter than its diff:
```python
import math

import jax
import jax.numpy as jnp
from jax import lax
from jax.experimental import pallas as pl
from jax.experimental.pallas import tpu as pltpu
from jax.sharding import PartitionSpec as P

MESH = pl.DeviceIdType.MESH
BF16 = jnp.bfloat16
F32 = jnp.float32

MEMBERS = 16
BANDS = 16
VARS = 72
PAD_VARS = 80
LONS = 512
CHANS = 256
OWNERS = 12
CHUNK = 48
RAW = VARS * 8
TAP_ROWS = 9 * VARS
PIECES = 21
PIECE = 32
STEPS = sorted(
    ((dx, dy) for dx in range(4) for dy in range(4)),
    key=lambda s: -(min(s[0], 4 - s[0]) + min(s[1], 4 - s[1])),
)


def kernel(
    members_ref, obs_ref, feats_ref, weight_ref, lat_ref, var_ref, land_ref,
    fg_ref, gw_ref,
    mbuf, obuf, gbuf, gf, obs, lats, vars_, land, fraw, ff, fs, wraw, weight, stack, wg, wgin, pieces, rs, zb, total,
    exch_send, exch_recv, back_send, back_recv, feat_send, feat_recv, halo_send, halo_recv, core_send, core_recv,
    rs_send, rs_recv, zb_send, zb_recv, ag_send, ag_recv, fwd_send, fwd_recv, load_sem,
    dp_in, one_in, two_in, four_in,
):
    ens = lax.axis_index("ens")
    lat = lax.axis_index("lat")
    dp = lax.axis_index("dp")
    core = lax.rem(ens, 2)
    x = lax.rem(ens, 8) // 2
    ylo = ens // 8
    y = dp * 2 + ylo
    up = lax.rem(lat + 1, BANDS)
    down = lax.rem(lat + BANDS - 1, BANDS)
    parity = lax.rem(lat, 2)
    pair = lat + 1 - 2 * parity
    other_core = ens + 1 - 2 * core

    def band(step):
        return lax.rem(lat + step, BANDS)

    def tell(sem, device):
        pl.semaphore_signal(sem, inc=1, device_id=device, device_id_type=MESH)

    barrier = pltpu.get_barrier_semaphore()

    def greet(k, c):
        tell(barrier, (lax.rem(ens + k, MEMBERS), lat, dp))
        return c

    lax.fori_loop(1, MEMBERS, greet, 0)
    tell(barrier, (ens, up, dp))
    tell(barrier, (ens, down, dp))
    tell(barrier, (ens, lat, 1 - dp))

    def chunk_of(e):
        pos = lax.rem(e, 4)
        first = jnp.where(e < 8, 1, 3)
        owns = pos != first
        return owns, (e // 4) * 3 + pos - jnp.where(pos > first, 1, 0)

    owned, mine = chunk_of(ens)
    mine = jnp.where(owned, mine, 0)

    loads = [
        pltpu.make_async_copy(src, dst, load_sem.at[i])
        for i, (src, dst) in enumerate((
            (feats_ref, fraw),
            (obs_ref.at[pl.ds(mine * CHUNK, CHUNK)], obs),
            (weight_ref, wraw),
            (land_ref, land),
            (lat_ref, lats),
            (var_ref, vars_),
        ))
    ]
    for load in loads:
        load.start()

    pl.semaphore_wait(barrier, 15 + 3)

    for dx, dy in STEPS:
        if dy > 1:
            continue
        for dc in range(2):
            if dx == dy == dc == 0:
                continue
            to = lax.rem(ylo + dy, 2) * 8 + lax.rem(x + dx, 4) * 2 + lax.rem(core + dc, 2)
            owns, chunk = chunk_of(to)

            @pl.when(owns)
            def _(to=to, chunk=chunk):
                pltpu.make_async_remote_copy(
                    src_ref=members_ref.at[pl.ds(chunk * CHUNK, CHUNK)], dst_ref=mbuf.at[ens],
                    send_sem=exch_send, recv_sem=exch_recv,
                    device_id=(to, lat, dp), device_id_type=MESH,
                ).start()

    @pl.when(owned)
    def _():
        pltpu.make_async_copy(members_ref.at[pl.ds(mine * CHUNK, CHUNK)], mbuf.at[ens], exch_recv).start()

    tell(dp_in, (ens, lat, 1 - dp))

    loads[0].wait()
    ff[...] = fraw[...].astype(F32)
    rows_out = []
    for r in range(2):
        for l in range(4):
            fs[r + 1, :, l * 128:(l + 1) * 128] = ff[pl.ds(2 * l + r, CHANS, stride=8), :].astype(BF16)
        rows_out.append(pltpu.make_async_remote_copy(
            src_ref=fs.at[r + 1], dst_ref=fs.at[3 - 3 * r],
            send_sem=feat_send.at[r], recv_sem=feat_recv.at[r],
            device_id=(ens, down if r == 0 else up, dp), device_id_type=MESH,
        ))
        rows_out[r].start()
    for load in loads[1:]:
        load.wait()

    @pl.when(owned)
    def _():
        pltpu.make_async_copy(mbuf, mbuf, exch_recv).wait()

        one = jnp.ones((16, 128), F32)
        zero = jnp.zeros((16, 128), F32)
        row = lax.broadcasted_iota(jnp.int32, (8, 128), 0)
        lat_rows = jnp.where(lax.rem(row, 2) == 0, lats[0], lats[1])
        land_rows = 1.0 + land[...].astype(F32)

        def tile(u, c):
            rows = pl.ds(pl.multiple_of(u * 16, 16), 16)
            vals = [mbuf[m, rows, :].astype(F32) for m in range(MEMBERS)]
            sums = [None] * MEMBERS
            for i in range(MEMBERS):
                for j in range(i + 1, MEMBERS):
                    s = jnp.where(vals[i] > vals[j], one, jnp.where(vals[i] < vals[j], -one, zero))
                    sums[i] = s if sums[i] is None else sums[i] + s
                    sums[j] = -s if sums[j] is None else sums[j] - s
            seen = obs[rows, :]
            v0 = mine * 6 + u * 2
            cell = jnp.concatenate(
                [(lat_rows * vars_[v0]) * land_rows, (lat_rows * vars_[v0 + 1]) * land_rows], axis=0
            )
            for m in range(MEMBERS):
                s = jnp.where(vals[m] > seen, one, jnp.where(vals[m] < seen, -one, zero))
                obuf[m, rows, :] = (cell * (s - sums[m] / (MEMBERS - 1))).astype(BF16)
            return c

        lax.fori_loop(0, CHUNK // 16, tile, 0)

        for dx, dy in STEPS:
            if dy > 1:
                continue
            for dc in range(2):
                if dx == dy == dc == 0:
                    continue
                to = lax.rem(ylo + dy, 2) * 8 + lax.rem(x + dx, 4) * 2 + lax.rem(core + dc, 2)
                pltpu.make_async_remote_copy(
                    src_ref=obuf.at[to], dst_ref=gbuf.at[pl.ds(mine * CHUNK, CHUNK)],
                    send_sem=back_send, recv_sem=back_recv,
                    device_id=(to, lat, dp), device_id_type=MESH,
                ).start()
        pltpu.make_async_copy(obuf.at[ens], gbuf.at[pl.ds(mine * CHUNK, CHUNK)], back_recv).start()

    pl.semaphore_wait(dp_in, 1)
    tell(one_in, (ens, up, dp))
    tell(one_in, (ens, down, dp))

    for t in range(9):
        taps = jnp.concatenate(
            [wraw[8 - t].astype(F32), jnp.zeros((PAD_VARS - VARS, CHANS), F32)], axis=0
        )
        weight[t * PAD_VARS:(t + 1) * PAD_VARS, :] = taps.astype(BF16)

    pltpu.make_async_copy(gbuf, gbuf, back_recv).wait()

    col = lax.broadcasted_iota(jnp.int32, (PAD_VARS, LONS), 1)

    def shifts(slot, v):
        stack[slot, 0] = jnp.where(col == 0, 0.0, pltpu.roll(v, 1, 1)).astype(BF16)
        stack[slot, 2] = jnp.where(col == LONS - 1, 0.0, pltpu.roll(v, LONS - 1, 1)).astype(BF16)

    gf[...] = gbuf[...].astype(F32)
    halo = []
    for r in range(2):
        v = jnp.concatenate([gf[pl.ds(2 * l + r, VARS, stride=8), :] for l in range(4)], axis=1)
        v = jnp.concatenate([v, jnp.zeros((PAD_VARS - VARS, LONS), F32)], axis=0)
        stack[r + 1, 1] = v.astype(BF16)
        halo.append(pltpu.make_async_remote_copy(
            src_ref=stack.at[r + 1, 1], dst_ref=stack.at[3 - 3 * r, 1],
            send_sem=halo_send.at[r], recv_sem=halo_recv.at[r],
            device_id=(ens, down if r == 0 else up, dp), device_id_type=MESH,
        ))
        halo[r].start()
        shifts(r + 1, v)
    pl.semaphore_wait(one_in, 2)
    tell(two_in, (ens, band(2), dp))
    tell(two_in, (ens, band(BANDS - 2), dp))

    def half(out, h, a):
        acc = None
        for r in range(2):
            part = lax.dot_general(
                stack[r + 1].reshape(3 * PAD_VARS, LONS),
                fs[r + 1 + a, pl.ds(pl.multiple_of(h * 128, 128), 128), :],
                (((1,), (1,)), ((), ())), preferred_element_type=F32,
            )
            acc = part if acc is None else acc + part
        for b in range(3):
            wg[out, a + 1, (2 - b) * VARS:(3 - b) * VARS, :] = acc[b * PAD_VARS:b * PAD_VARS + VARS, :]

    to_core = []
    for a in (0, -1, 1):
        if a:
            rows_out[(1 + a) // 2 ^ 1].wait_recv()

            @pl.when(lat == (0 if a < 0 else BANDS - 1))
            def _(a=a):
                fs[0 if a < 0 else 3] = jnp.zeros((CHANS, LONS), BF16)

        half(0, 1 - core, a)
        copy = pltpu.make_async_remote_copy(
            src_ref=wg.at[0, a + 1], dst_ref=wgin.at[a + 1], send_sem=core_send.at[a + 1], recv_sem=core_recv.at[a + 1],
            device_id=(other_core, lat, dp), device_id_type=MESH,
        )
        copy.start()
        to_core.append(copy)
    for a in (0, -1, 1):
        half(1, core, a)
    pl.semaphore_wait(two_in, 2)
    tell(four_in, (ens, band(4), dp))
    tell(four_in, (ens, band(BANDS - 4), dp))
    for copy in to_core:
        copy.wait_recv()
    mine_sum = (wg[1] + wgin[...]).reshape(TAP_ROWS, 128)
    fill = jnp.zeros((PIECES * PIECE - TAP_ROWS, 128), F32)
    pieces[...] = jnp.concatenate([mine_sum, fill], axis=0).astype(BF16)

    def piece_of(chip, par):
        first = lax.rem(lax.rem(chip, 4) + chip // 4, 2) == par
        second = jnp.logical_and(lax.rem(chip, 3) == 0, chip < 15)
        return jnp.logical_or(first, second), jnp.where(first, chip, 16 + chip // 3)

    spots = []
    for dz in (1, 0):
        for dx, dy in STEPS:
            if dx == dy == dz == 0:
                continue
            qx = lax.rem(x + dx, 4)
            qy = lax.rem(y + dy, 4)
            par = parity if dz == 0 else 1 - parity
            device = (lax.rem(qy, 2) * 8 + qx * 2 + core, lat if dz == 0 else pair, qy // 2)
            spots.append((qy * 4 + qx, par, device))
    place = (y * 4 + x) * 2 + parity
    sums, piece = piece_of(y * 4 + x, parity)
    piece = jnp.where(sums, piece, 0)
    for chip, par, device in spots:
        theirs, q = piece_of(chip, par)

        @pl.when(theirs)
        def _(q=q, device=device):
            pltpu.make_async_remote_copy(
                src_ref=pieces.at[pl.ds(q * PIECE, PIECE)], dst_ref=rs.at[place],
                send_sem=rs_send, recv_sem=rs_recv, device_id=device, device_id_type=MESH,
            ).start()

    @pl.when(sums)
    def _():
        pltpu.make_async_copy(pieces.at[pl.ds(piece * PIECE, PIECE)], rs.at[place], rs_recv).start()

    for r in range(2):
        halo[r].wait_recv()
    for slot, edge in ((3, BANDS - 1), (0, 0)):
        v = jnp.where(lat == edge, 0.0, stack[slot, 1].astype(F32))
        stack[slot, 1] = v.astype(BF16)
        shifts(slot, v)
    for r in range(2):
        grad = lax.dot_general(
            weight[...], stack[pl.ds(r, 3)].reshape(9 * PAD_VARS, LONS),
            (((0,), (0,)), ((), ())), preferred_element_type=F32,
        )
        for l in range(4):
            ff[pl.ds(2 * l + r, CHANS, stride=8), :] = grad[:, l * 128:(l + 1) * 128]
    fraw[...] = ff[...].astype(BF16)
    store = pltpu.make_async_copy(fraw, fg_ref, load_sem.at[0])
    store.start()

    pl.semaphore_wait(four_in, 2)

    @pl.when(sums)
    def _():
        pltpu.make_async_copy(rs, rs, rs_recv).wait()
        acc = rs[0].astype(F32)
        for q in range(1, 32):
            acc = acc + rs[q].astype(F32)
        zb[lat // 2] = acc.astype(BF16)
        for k in (8, 6, 10, 4, 12, 2, 14):
            pltpu.make_async_remote_copy(
                src_ref=zb.at[lat // 2], dst_ref=zb.at[lat // 2], send_sem=zb_send, recv_sem=zb_recv,
                device_id=(ens, band(k), dp), device_id_type=MESH,
            ).start()
        pltpu.make_async_copy(zb.at[pl.ds(0, 7)], zb.at[pl.ds(0, 7)], zb_recv).wait()
        acc = zb[0].astype(F32)
        for q in range(1, 8):
            acc = acc + zb[q].astype(F32)
        total[...] = acc.astype(BF16)
        for _, _, device in spots:
            pltpu.make_async_remote_copy(
                src_ref=total, dst_ref=gw_ref.at[core, piece],
                send_sem=ag_send, recv_sem=ag_recv, device_id=device, device_id_type=MESH,
            ).start()
        pltpu.make_async_copy(total, gw_ref.at[core, piece], ag_recv).start()

    pltpu.make_async_copy(gw_ref.at[core], gw_ref.at[core], ag_recv).wait()
    forward = pltpu.make_async_remote_copy(
        src_ref=gw_ref.at[core], dst_ref=gw_ref.at[core], send_sem=fwd_send, recv_sem=fwd_recv,
        device_id=(other_core, lat, dp), device_id_type=MESH,
    )
    forward.start()

    @pl.when(owned)
    def _():
        pltpu.make_async_copy(mbuf.at[pl.ds(0, OWNERS - 1)], mbuf.at[pl.ds(0, OWNERS - 1)], exch_send).wait()
        pltpu.make_async_copy(obuf.at[pl.ds(0, MEMBERS - 1)], obuf.at[pl.ds(0, MEMBERS - 1)], back_send).wait()

    @pl.when(jnp.logical_not(owned))
    def _():
        pltpu.make_async_copy(mbuf.at[pl.ds(0, OWNERS)], mbuf.at[pl.ds(0, OWNERS)], exch_send).wait()

    for r in range(2):
        rows_out[r].wait_send()
        halo[r].wait_send()
    for copy in to_core:
        copy.wait_send()

    @pl.when(sums)
    def _():
        pltpu.make_async_copy(rs.at[pl.ds(0, PIECES - 1)], rs.at[pl.ds(0, PIECES - 1)], rs_send).wait()
        pltpu.make_async_copy(zb.at[pl.ds(0, 7)], zb.at[pl.ds(0, 7)], zb_send).wait()
        pltpu.make_async_copy(rs.at[pl.ds(0, 31)], rs.at[pl.ds(0, 31)], ag_send).wait()

    @pl.when(jnp.logical_not(sums))
    def _():
        pltpu.make_async_copy(rs.at[pl.ds(0, PIECES)], rs.at[pl.ds(0, PIECES)], rs_send).wait()

    store.wait()
    forward.wait()


def write_results(factor, fg_ref, gw_ref, fg_out, gw_out, fgbuf, gwbuf, outbuf, sems, load_sem, fg_sems):
    load = pltpu.make_async_copy(gw_ref, gwbuf, load_sem)
    load.start()
    quarter = CHANS * 2
    parts = [pl.ds(i * quarter, quarter) for i in range(4)]
    loads = [pltpu.make_async_copy(fg_ref.at[p], fgbuf.at[p], fg_sems.at[i]) for i, p in enumerate(parts)]
    for copy in loads:
        copy.start()
    load.wait()
    copies = []
    for i in range(3):
        rows = pl.ds(i * 3 * VARS, 3 * VARS)
        for c in range(2):
            wide = gwbuf[c].reshape(PIECES * PIECE, 128).astype(F32)
            outbuf[rows, c * 128:(c + 1) * 128] = wide[i * 3 * VARS:(i + 1) * 3 * VARS] * factor
        copies.append(pltpu.make_async_copy(outbuf.at[rows], gw_out.at[rows], sems.at[i]))
        copies[i].start()
    for i, p in enumerate(parts):
        loads[i].wait()
        copies.append(pltpu.make_async_copy(fgbuf.at[p], fg_out.at[p], sems.at[3 + i]))
        copies[-1].start()
    for copy in copies:
        copy.wait()


def raw_rows(v):
    lead = v.shape[0]
    return v.reshape(lead, 2, 4, 128).transpose(0, 2, 1, 3).reshape(lead * 8, 128)


def local(features, members_out, observed, conv_weight, lat_weight, var_weight, land_mask):
    hbm = pl.BlockSpec(memory_space=pltpu.HBM)
    anywhere = pl.BlockSpec(memory_space=pl.ANY)
    dma = pltpu.SemaphoreType.DMA
    regular = pltpu.SemaphoreType.REGULAR
    fg, gw = pl.pallas_call(
        kernel,
        out_shape=(
            jax.ShapeDtypeStruct((CHANS * 8, 128), BF16),
            jax.ShapeDtypeStruct((2, PIECES, PIECE, 128), BF16),
        ),
        in_specs=[hbm] * 7,
        out_specs=(anywhere, anywhere),
        scratch_shapes=[
            pltpu.VMEM((MEMBERS, CHUNK, 128), BF16),
            pltpu.VMEM((MEMBERS, CHUNK, 128), BF16),
            pltpu.VMEM((RAW, 128), BF16),
            pltpu.VMEM((RAW, 128), F32),
            pltpu.VMEM((CHUNK, 128), F32),
            pltpu.SMEM((2,), F32),
            pltpu.SMEM((VARS,), F32),
            pltpu.VMEM((8, 128), jnp.int32),
            pltpu.VMEM((CHANS * 8, 128), BF16),
            pltpu.VMEM((CHANS * 8, 128), F32),
            pltpu.VMEM((4, CHANS, LONS), BF16),
            pltpu.VMEM((9, VARS, CHANS), BF16),
            pltpu.VMEM((9 * PAD_VARS, CHANS), BF16),
            pltpu.VMEM((4, 3, PAD_VARS, LONS), BF16),
            pltpu.VMEM((2, 3, 3 * VARS, 128), F32),
            pltpu.VMEM((3, 3 * VARS, 128), F32),
            pltpu.VMEM((PIECES * PIECE, 128), BF16),
            pltpu.VMEM((32, PIECE, 128), BF16),
            pltpu.VMEM((8, PIECE, 128), BF16),
            pltpu.VMEM((PIECE, 128), BF16),
            dma, dma, dma, dma, dma((2,)), dma((2,)), dma((2,)), dma((2,)), dma((3,)), dma((3,)),
            dma, dma, dma, dma, dma, dma, dma, dma, dma((6,)),
            regular, regular, regular, regular,
        ],
        compiler_params=pltpu.CompilerParams(
            collective_id=0, has_side_effects=True, vmem_limit_bytes=60 * 1024 * 1024
        ),
        name="crps_backward",
    )(
        raw_rows(members_out[0, 0]), raw_rows(observed[0]), raw_rows(features[0, 0]), conv_weight,
        lat_weight, var_weight, raw_rows(land_mask[None]),
    )
    factor = 1.0 / math.sqrt(2 * MEMBERS * 32 * LONS)

    def body(*refs):
        write_results(factor, *refs)

    feature_grad, grad_weight = pl.pallas_call(
        body,
        out_shape=(
            jax.ShapeDtypeStruct((CHANS * 8, 128), BF16),
            jax.ShapeDtypeStruct((TAP_ROWS, CHANS), F32),
        ),
        in_specs=[anywhere, anywhere],
        out_specs=(hbm, hbm),
        scratch_shapes=[
            pltpu.VMEM((CHANS * 8, 128), BF16),
            pltpu.VMEM((2, PIECES, PIECE, 128), BF16),
            pltpu.VMEM((TAP_ROWS, CHANS), F32),
            dma((7,)), dma, dma((4,)),
        ],
        compiler_params=pltpu.CompilerParams(vmem_limit_bytes=60 * 1024 * 1024),
        name="write_results",
    )(fg, gw)
    feature_grad = feature_grad.reshape(CHANS, 4, 2, 128).transpose(0, 2, 1, 3).reshape(1, 1, CHANS, 2, LONS)
    return (feature_grad, grad_weight.reshape(9, VARS, CHANS))


def solution(mesh):
    return jax.shard_map(
        local,
        mesh=mesh,
        in_specs=(
            P("dp", "ens", None, "lat", None),
            P("dp", "ens", None, "lat", None),
            P("dp", None, "lat", None),
            P(),
            P("lat"),
            P(),
            P("lat", None),
        ),
        out_specs=(P("dp", "ens", None, "lat", None), P()),
        check_vma=False,
    )
```

time: 548 us -> 50.4 us (0.09)
  waiting for transfers between devices: 514 us -> 0 us
  Pallas kernels: 0 us -> 49.6 us
  between operations: 14.3 us -> 0.64 us
  other arithmetic: 8.11 us -> 0 us
    psum x1 -> x0, waiting for transfers between devices: 463 us -> none  [local(): summed = lax.psum(weight_grad, ('ens', 'lat', 'dp'))]
    pallas_call x0 -> x2, Pallas kernels: none -> 49.6 us  [the longest x1 47.3 us: local(): pl.pallas_call(kernel, out_shape=(jax.ShapeDtypeStruct((CHANS * 8, 128),...]
    all_gather x1 -> x0, waiting for transfers between devices: 47.2 us -> none  [local(): lax.all_gather(members_out, 'ens', axis=1, tiled=True)[0]]
  transfers between devices with their start and end apart: 4 -> 0, of which waited for: 3 -> 0; matrix products, arithmetic and copies ran while one was open for 1% -> 0% of each run, Pallas kernels for 0% -> 0%
where the time goes in v2:
time: 50.4 us; the launch traced here: 50.3 us
  Pallas kernels  49.6 us (98%)
  between operations  0.64 us (1%)
    pallas_call x1, Pallas kernels, local(): pl.pallas_call(kernel, out_shape=(jax.ShapeDtypeStruct((CHANS * 8, 128),...  47.3 us
    pallas_call x1, Pallas kernels, local(): pl.pallas_call(body, out_shape=(jax.ShapeDtypeStruct((CHANS * 8, 128), BF...  2.3 us

profile of v2, /device:TPU:1, one launch (start us, length us, event | category | flops | bytes accessed | tf_op | source)
XLA Modules:
  0.0 50.3 jit_solution(17955458402688933508)
XLA Ops:
  0.6 47.3 %crps_backward.1 = (bf16[2048,128]{1,0:T(8,128)(2,1)}, bf16[2,21,32,128]{3,2,1,0:T(8,128)(2,1)}) custom-call(bf16[576,128]{1,0:T(8,128)(2,1)} %bitcast.28, f32[576,128]{1,0:T(8,128)} %bitcast.27, bf16[2048,128]{1,0:T(8,128)(2,1)} %bitcast.26, bf16[9,72,256]{2,1,0:T(8,128)(2,1)} %weight_ref.1, f32[2]{0:T(128)} %lat_ref.1, f32[72]{0:T(128)} %var_ref.1, ...), custom_call_target="tpu_custom_call" | custom-call | tf_op jit(solution)/shard_map/crps_backward/pallas_call | solution.py:398
  48.0 2.3 %write_results.1 = (bf16[2048,128]{1,0:T(8,128)(2,1)}, f32[648,256]{1,0:T(8,128)}) custom-call(bf16[2048,128]{1,0:T(8,128)(2,1)} %get-tuple-element.6.refs_0_, bf16[2,21,32,128]{3,2,1,0:T(8,128)(2,1)} %get-tuple-element.7.refs_1_), custom_call_target="tpu_custom_call" | custom-call | tf_op jit(solution)/shard_map/write_results/pallas_call | solution.py:444

commit v3 on v2

--- a/solution.py
+++ b/solution.py
@@ -32,10 +32,10 @@
 def kernel(
     members_ref, obs_ref, feats_ref, weight_ref, lat_ref, var_ref, land_ref,
     fg_ref, gw_ref,
-    mbuf, obuf, gbuf, gf, obs, lats, vars_, land, fraw, ff, fs, wraw, weight, stack, wg, wgin, pieces, rs, zb, total,
+    members, mbuf, obuf, gbuf, gf, obs, lats, vars_, land, fraw, ff, fs, wraw, weight, stack, wg, wgin, pieces, rs, zb, total,
     exch_send, exch_recv, back_send, back_recv, feat_send, feat_recv, halo_send, halo_recv, core_send, core_recv,
     rs_send, rs_recv, zb_send, zb_recv, ag_send, ag_recv, fwd_send, fwd_recv, load_sem,
-    dp_in, one_in, two_in, four_in,
+    dp_in, pair_in, one_in, two_in, four_in,
 ):
     ens = lax.axis_index("ens")
     lat = lax.axis_index("lat")
@@ -79,6 +79,7 @@
     loads = [
         pltpu.make_async_copy(src, dst, load_sem.at[i])
         for i, (src, dst) in enumerate((
+            (members_ref, members),
             (feats_ref, fraw),
             (obs_ref.at[pl.ds(mine * CHUNK, CHUNK)], obs),
             (weight_ref, wraw),
@@ -89,6 +90,7 @@
     ]
     for load in loads:
         load.start()
+    loads[0].wait()
 
     pl.semaphore_wait(barrier, 15 + 3)
 
@@ -104,18 +106,20 @@
             @pl.when(owns)
             def _(to=to, chunk=chunk):
                 pltpu.make_async_remote_copy(
-                    src_ref=members_ref.at[pl.ds(chunk * CHUNK, CHUNK)], dst_ref=mbuf.at[ens],
+                    src_ref=members.at[pl.ds(chunk * CHUNK, CHUNK)], dst_ref=mbuf.at[ens],
                     send_sem=exch_send, recv_sem=exch_recv,
                     device_id=(to, lat, dp), device_id_type=MESH,
                 ).start()
 
     @pl.when(owned)
     def _():
-        pltpu.make_async_copy(members_ref.at[pl.ds(mine * CHUNK, CHUNK)], mbuf.at[ens], exch_recv).start()
+        pltpu.make_async_copy(members.at[pl.ds(mine * CHUNK, CHUNK)], mbuf.at[ens], exch_recv).start()
 
     tell(dp_in, (ens, lat, 1 - dp))
-
-    loads[0].wait()
+    tell(one_in, (ens, up, dp))
+    tell(one_in, (ens, down, dp))
+
+    loads[1].wait()
     ff[...] = fraw[...].astype(F32)
     rows_out = []
     for r in range(2):
@@ -127,8 +131,11 @@
             device_id=(ens, down if r == 0 else up, dp), device_id_type=MESH,
         ))
         rows_out[r].start()
-    for load in loads[1:]:
+    for load in loads[2:]:
         load.wait()
+    pl.semaphore_wait(one_in, 2)
+    tell(two_in, (ens, band(2), dp))
+    tell(two_in, (ens, band(BANDS - 2), dp))
 
     @pl.when(owned)
     def _():
@@ -176,8 +183,10 @@
         pltpu.make_async_copy(obuf.at[ens], gbuf.at[pl.ds(mine * CHUNK, CHUNK)], back_recv).start()
 
     pl.semaphore_wait(dp_in, 1)
-    tell(one_in, (ens, up, dp))
-    tell(one_in, (ens, down, dp))
+    tell(pair_in, (ens, pair, dp))
+    pl.semaphore_wait(two_in, 2)
+    tell(four_in, (ens, band(4), dp))
+    tell(four_in, (ens, band(BANDS - 4), dp))
 
     for t in range(9):
         taps = jnp.concatenate(
@@ -206,9 +215,6 @@
         ))
         halo[r].start()
         shifts(r + 1, v)
-    pl.semaphore_wait(one_in, 2)
-    tell(two_in, (ens, band(2), dp))
-    tell(two_in, (ens, band(BANDS - 2), dp))
 
     def half(out, h, a):
         acc = None
@@ -240,9 +246,7 @@
         to_core.append(copy)
     for a in (0, -1, 1):
         half(1, core, a)
-    pl.semaphore_wait(two_in, 2)
-    tell(four_in, (ens, band(4), dp))
-    tell(four_in, (ens, band(BANDS - 4), dp))
+    pl.semaphore_wait(pair_in, 1)
     for copy in to_core:
         copy.wait_recv()
     mine_sum = (wg[1] + wgin[...]).reshape(TAP_ROWS, 128)
@@ -294,9 +298,7 @@
         )
         for l in range(4):
             ff[pl.ds(2 * l + r, CHANS, stride=8), :] = grad[:, l * 128:(l + 1) * 128]
-    fraw[...] = ff[...].astype(BF16)
-    store = pltpu.make_async_copy(fraw, fg_ref, load_sem.at[0])
-    store.start()
+    fg_ref[...] = ff[...].astype(BF16)
 
     pl.semaphore_wait(four_in, 2)
 
@@ -356,30 +358,18 @@
     def _():
         pltpu.make_async_copy(rs.at[pl.ds(0, PIECES)], rs.at[pl.ds(0, PIECES)], rs_send).wait()
 
-    store.wait()
     forward.wait()
 
 
-def write_results(factor, fg_ref, gw_ref, fg_out, gw_out, fgbuf, gwbuf, outbuf, sems, load_sem, fg_sems):
-    load = pltpu.make_async_copy(gw_ref, gwbuf, load_sem)
-    load.start()
-    quarter = CHANS * 2
-    parts = [pl.ds(i * quarter, quarter) for i in range(4)]
-    loads = [pltpu.make_async_copy(fg_ref.at[p], fgbuf.at[p], fg_sems.at[i]) for i, p in enumerate(parts)]
-    for copy in loads:
-        copy.start()
-    load.wait()
-    copies = []
+def write_results(factor, fg_ref, gw_ref, fg_out, gw_out, outbuf, sems):
+    copies = [pltpu.make_async_copy(fg_ref, fg_out, sems.at[3])]
+    copies[0].start()
     for i in range(3):
         rows = pl.ds(i * 3 * VARS, 3 * VARS)
         for c in range(2):
-            wide = gwbuf[c].reshape(PIECES * PIECE, 128).astype(F32)
+            wide = gw_ref[c].reshape(PIECES * PIECE, 128).astype(F32)
             outbuf[rows, c * 128:(c + 1) * 128] = wide[i * 3 * VARS:(i + 1) * 3 * VARS] * factor
         copies.append(pltpu.make_async_copy(outbuf.at[rows], gw_out.at[rows], sems.at[i]))
-        copies[i].start()
-    for i, p in enumerate(parts):
-        loads[i].wait()
-        copies.append(pltpu.make_async_copy(fgbuf.at[p], fg_out.at[p], sems.at[3 + i]))
         copies[-1].start()
     for copy in copies:
         copy.wait()
@@ -392,18 +382,19 @@
 
 def local(features, members_out, observed, conv_weight, lat_weight, var_weight, land_mask):
     hbm = pl.BlockSpec(memory_space=pltpu.HBM)
-    anywhere = pl.BlockSpec(memory_space=pl.ANY)
+    vmem = pl.BlockSpec(memory_space=pltpu.VMEM)
     dma = pltpu.SemaphoreType.DMA
     regular = pltpu.SemaphoreType.REGULAR
     fg, gw = pl.pallas_call(
         kernel,
         out_shape=(
-            jax.ShapeDtypeStruct((CHANS * 8, 128), BF16),
-            jax.ShapeDtypeStruct((2, PIECES, PIECE, 128), BF16),
+            pltpu.VMEM((CHANS * 8, 128), BF16),
+            pltpu.VMEM((2, PIECES, PIECE, 128), BF16),
         ),
         in_specs=[hbm] * 7,
-        out_specs=(anywhere, anywhere),
+        out_specs=(vmem, vmem),
         scratch_shapes=[
+            pltpu.VMEM((RAW, 128), BF16),
             pltpu.VMEM((MEMBERS, CHUNK, 128), BF16),
             pltpu.VMEM((MEMBERS, CHUNK, 128), BF16),
             pltpu.VMEM((RAW, 128), BF16),
@@ -425,17 +416,20 @@
             pltpu.VMEM((8, PIECE, 128), BF16),
             pltpu.VMEM((PIECE, 128), BF16),
             dma, dma, dma, dma, dma((2,)), dma((2,)), dma((2,)), dma((2,)), dma((3,)), dma((3,)),
-            dma, dma, dma, dma, dma, dma, dma, dma, dma((6,)),
-            regular, regular, regular, regular,
+            dma, dma, dma, dma, dma, dma, dma, dma, dma((7,)),
+            regular, regular, regular, regular, regular,
         ],
         compiler_params=pltpu.CompilerParams(
-            collective_id=0, has_side_effects=True, vmem_limit_bytes=60 * 1024 * 1024
+            collective_id=0, has_side_effects=True, vmem_limit_bytes=48 * 1024 * 1024
         ),
         name="crps_backward",
-    )(
-        raw_rows(members_out[0, 0]), raw_rows(observed[0]), raw_rows(features[0, 0]), conv_weight,
-        lat_weight, var_weight, raw_rows(land_mask[None]),
-    )
+    )(*(
+        pltpu.with_memory_space_constraint(v, pltpu.HBM)
+        for v in (
+            raw_rows(members_out[0, 0]), raw_rows(observed[0]), raw_rows(features[0, 0]), conv_weight,
+            lat_weight, var_weight, raw_rows(land_mask[None]),
+        )
+    ))
     factor = 1.0 / math.sqrt(2 * MEMBERS * 32 * LONS)
 
     def body(*refs):
@@ -447,17 +441,15 @@
             jax.ShapeDtypeStruct((CHANS * 8, 128), BF16),
             jax.ShapeDtypeStruct((TAP_ROWS, CHANS), F32),
         ),
-        in_specs=[anywhere, anywhere],
+        in_specs=[vmem, vmem],
         out_specs=(hbm, hbm),
         scratch_shapes=[
-            pltpu.VMEM((CHANS * 8, 128), BF16),
-            pltpu.VMEM((2, PIECES, PIECE, 128), BF16),
             pltpu.VMEM((TAP_ROWS, CHANS), F32),
-            dma((7,)), dma, dma((4,)),
+            dma((4,)),
         ],
-        compiler_params=pltpu.CompilerParams(vmem_limit_bytes=60 * 1024 * 1024),
+        compiler_params=pltpu.CompilerParams(vmem_limit_bytes=48 * 1024 * 1024),
         name="write_results",
-    )(fg, gw)
+    )(*(pltpu.with_memory_space_constraint(v, pltpu.VMEM) for v in (fg, gw)))
     feature_grad = feature_grad.reshape(CHANS, 4, 2, 128).transpose(0, 2, 1, 3).reshape(1, 1, CHANS, 2, LONS)
     return (feature_grad, grad_weight.reshape(9, VARS, CHANS))
 

time: 50.4 us -> 48.5 us (0.962)
  Pallas kernels: 49.6 us -> 47.7 us
    pallas_call x1, Pallas kernels: 2.3 us -> 1.04 us  [local(): pl.pallas_call(body, out_shape=(jax.ShapeDtypeStruct((CHANS * 8, 128), BF...]
    pallas_call x1, Pallas kernels: 47.3 us -> 46.6 us  [local(): pl.pallas_call(kernel, out_shape=(pltpu.VMEM((CHANS * 8, 128), BF16), plt...]
where the time goes in v3:
time: 48.5 us; the launch traced here: 48.3 us
  Pallas kernels  47.7 us (98%)
  between operations  0.64 us (1%)
    pallas_call x1, Pallas kernels, local(): pl.pallas_call(kernel, out_shape=(pltpu.VMEM((CHANS * 8, 128), BF16), plt...  46.6 us
    pallas_call x1, Pallas kernels, local(): pl.pallas_call(body, out_shape=(jax.ShapeDtypeStruct((CHANS * 8, 128), BF...  1.04 us

profile of v3, /device:TPU:1, one launch (start us, length us, event | category | flops | bytes accessed | tf_op | source)
XLA Modules:
  0.0 48.3 jit_solution(1866285902630218222)
XLA Ops:
  0.6 46.6 %crps_backward.1 = (bf16[2048,128]{1,0:T(8,128)(2,1)S(1)}, bf16[2,21,32,128]{3,2,1,0:T(8,128)(2,1)S(1)}) custom-call(bf16[576,128]{1,0:T(8,128)(2,1)} %bitcast.28, f32[576,128]{1,0:T(8,128)} %bitcast.27, bf16[2048,128]{1,0:T(8,128)(2,1)} %bitcast.26, bf16[9,72,256]{2,1,0:T(8,128)(2,1)} %weight_ref.1, f32[2]{0:T(128)} %lat_ref.1, f32[72]{0:T(128)} %var_ref.1, ...), custom_call_target="tpu_custom_call" | custom-call | tf_op jit(solution)/shard_map/crps_backward/pallas_call | solution.py:388
  47.3 1.0 %write_results.1 = (bf16[2048,128]{1,0:T(8,128)(2,1)}, f32[648,256]{1,0:T(8,128)}) custom-call(bf16[2048,128]{1,0:T(8,128)(2,1)S(1)} %get-tuple-element.6.refs_0_, bf16[2,21,32,128]{3,2,1,0:T(8,128)(2,1)S(1)} %get-tuple-element.7.refs_1_), custom_call_target="tpu_custom_call" | custom-call | tf_op jit(solution)/shard_map/write_results/pallas_call | solution.py:438

commit v4 on v3

--- a/solution.py
+++ b/solution.py
@@ -29,6 +29,18 @@
 )
 
 
+def div(v, n):
+    return lax.shift_right_logical(v, n.bit_length() - 1)
+
+
+def mod(v, n):
+    return lax.bitwise_and(v, n - 1)
+
+
+def third(v):
+    return lax.shift_right_logical(v * 11, 5)
+
+
 def kernel(
     members_ref, obs_ref, feats_ref, weight_ref, lat_ref, var_ref, land_ref,
     fg_ref, gw_ref,
@@ -40,38 +52,37 @@
     ens = lax.axis_index("ens")
     lat = lax.axis_index("lat")
     dp = lax.axis_index("dp")
-    core = lax.rem(ens, 2)
-    x = lax.rem(ens, 8) // 2
-    ylo = ens // 8
+    core = mod(ens, 2)
+    x = div(mod(ens, 8), 2)
+    ylo = div(ens, 8)
     y = dp * 2 + ylo
-    up = lax.rem(lat + 1, BANDS)
-    down = lax.rem(lat + BANDS - 1, BANDS)
-    parity = lax.rem(lat, 2)
+    up = mod(lat + 1, BANDS)
+    down = mod(lat + BANDS - 1, BANDS)
+    parity = mod(lat, 2)
     pair = lat + 1 - 2 * parity
     other_core = ens + 1 - 2 * core
 
     def band(step):
-        return lax.rem(lat + step, BANDS)
+        return mod(lat + step, BANDS)
 
     def tell(sem, device):
         pl.semaphore_signal(sem, inc=1, device_id=device, device_id_type=MESH)
 
     barrier = pltpu.get_barrier_semaphore()
 
-    def greet(k, c):
-        tell(barrier, (lax.rem(ens + k, MEMBERS), lat, dp))
-        return c
-
-    lax.fori_loop(1, MEMBERS, greet, 0)
+    for dx, dy in STEPS:
+        for dc in range(2):
+            if dy <= 1 and (dx or dy or dc):
+                tell(barrier, (mod(ylo + dy, 2) * 8 + mod(x + dx, 4) * 2 + mod(core + dc, 2), lat, dp))
     tell(barrier, (ens, up, dp))
     tell(barrier, (ens, down, dp))
     tell(barrier, (ens, lat, 1 - dp))
 
     def chunk_of(e):
-        pos = lax.rem(e, 4)
+        pos = mod(e, 4)
         first = jnp.where(e < 8, 1, 3)
         owns = pos != first
-        return owns, (e // 4) * 3 + pos - jnp.where(pos > first, 1, 0)
+        return owns, div(e, 4) * 3 + pos - jnp.where(pos > first, 1, 0)
 
     owned, mine = chunk_of(ens)
     mine = jnp.where(owned, mine, 0)
@@ -100,7 +111,7 @@
         for dc in range(2):
             if dx == dy == dc == 0:
                 continue
-            to = lax.rem(ylo + dy, 2) * 8 + lax.rem(x + dx, 4) * 2 + lax.rem(core + dc, 2)
+            to = mod(ylo + dy, 2) * 8 + mod(x + dx, 4) * 2 + mod(core + dc, 2)
             owns, chunk = chunk_of(to)
 
             @pl.when(owns)
@@ -174,7 +185,7 @@
             for dc in range(2):
                 if dx == dy == dc == 0:
                     continue
-                to = lax.rem(ylo + dy, 2) * 8 + lax.rem(x + dx, 4) * 2 + lax.rem(core + dc, 2)
+                to = mod(ylo + dy, 2) * 8 + mod(x + dx, 4) * 2 + mod(core + dc, 2)
                 pltpu.make_async_remote_copy(
                     src_ref=obuf.at[to], dst_ref=gbuf.at[pl.ds(mine * CHUNK, CHUNK)],
                     send_sem=back_send, recv_sem=back_recv,
@@ -216,57 +227,55 @@
         halo[r].start()
         shifts(r + 1, v)
 
-    def half(out, h, a):
+    to_core = []
+    for a in (0, -1, 1):
+        if a:
+            rows_out[0 if a > 0 else 1].wait_recv()
+
+            @pl.when(lat == (0 if a < 0 else BANDS - 1))
+            def _(a=a):
+                fs[0 if a < 0 else 3] = jnp.zeros((CHANS, LONS), BF16)
+
         acc = None
         for r in range(2):
             part = lax.dot_general(
-                stack[r + 1].reshape(3 * PAD_VARS, LONS),
-                fs[r + 1 + a, pl.ds(pl.multiple_of(h * 128, 128), 128), :],
+                stack[r + 1].reshape(3 * PAD_VARS, LONS), fs[r + 1 + a],
                 (((1,), (1,)), ((), ())), preferred_element_type=F32,
             )
             acc = part if acc is None else acc + part
         for b in range(3):
-            wg[out, a + 1, (2 - b) * VARS:(3 - b) * VARS, :] = acc[b * PAD_VARS:b * PAD_VARS + VARS, :]
-
-    to_core = []
-    for a in (0, -1, 1):
-        if a:
-            rows_out[(1 + a) // 2 ^ 1].wait_recv()
-
-            @pl.when(lat == (0 if a < 0 else BANDS - 1))
-            def _(a=a):
-                fs[0 if a < 0 else 3] = jnp.zeros((CHANS, LONS), BF16)
-
-        half(0, 1 - core, a)
+            for h in range(2):
+                wg[h, a + 1, (2 - b) * VARS:(3 - b) * VARS, :] = acc[
+                    b * PAD_VARS:b * PAD_VARS + VARS, h * 128:(h + 1) * 128
+                ]
         copy = pltpu.make_async_remote_copy(
-            src_ref=wg.at[0, a + 1], dst_ref=wgin.at[a + 1], send_sem=core_send.at[a + 1], recv_sem=core_recv.at[a + 1],
+            src_ref=wg.at[1 - core, a + 1], dst_ref=wgin.at[a + 1],
+            send_sem=core_send.at[a + 1], recv_sem=core_recv.at[a + 1],
             device_id=(other_core, lat, dp), device_id_type=MESH,
         )
         copy.start()
         to_core.append(copy)
-    for a in (0, -1, 1):
-        half(1, core, a)
     pl.semaphore_wait(pair_in, 1)
     for copy in to_core:
         copy.wait_recv()
-    mine_sum = (wg[1] + wgin[...]).reshape(TAP_ROWS, 128)
+    mine_sum = (wg[core] + wgin[...]).reshape(TAP_ROWS, 128)
     fill = jnp.zeros((PIECES * PIECE - TAP_ROWS, 128), F32)
     pieces[...] = jnp.concatenate([mine_sum, fill], axis=0).astype(BF16)
 
     def piece_of(chip, par):
-        first = lax.rem(lax.rem(chip, 4) + chip // 4, 2) == par
-        second = jnp.logical_and(lax.rem(chip, 3) == 0, chip < 15)
-        return jnp.logical_or(first, second), jnp.where(first, chip, 16 + chip // 3)
+        first = mod(mod(chip, 4) + div(chip, 4), 2) == par
+        second = jnp.logical_and(chip == 3 * third(chip), chip < 15)
+        return jnp.logical_or(first, second), jnp.where(first, chip, 16 + third(chip))
 
     spots = []
     for dz in (1, 0):
         for dx, dy in STEPS:
             if dx == dy == dz == 0:
                 continue
-            qx = lax.rem(x + dx, 4)
-            qy = lax.rem(y + dy, 4)
+            qx = mod(x + dx, 4)
+            qy = mod(y + dy, 4)
             par = parity if dz == 0 else 1 - parity
-            device = (lax.rem(qy, 2) * 8 + qx * 2 + core, lat if dz == 0 else pair, qy // 2)
+            device = (mod(qy, 2) * 8 + qx * 2 + core, lat if dz == 0 else pair, div(qy, 2))
             spots.append((qy * 4 + qx, par, device))
     place = (y * 4 + x) * 2 + parity
     sums, piece = piece_of(y * 4 + x, parity)
@@ -308,22 +317,33 @@
         acc = rs[0].astype(F32)
         for q in range(1, 32):
             acc = acc + rs[q].astype(F32)
-        zb[lat // 2] = acc.astype(BF16)
-        for k in (8, 6, 10, 4, 12, 2, 14):
-            pltpu.make_async_remote_copy(
-                src_ref=zb.at[lat // 2], dst_ref=zb.at[lat // 2], send_sem=zb_send, recv_sem=zb_recv,
-                device_id=(ens, band(k), dp), device_id_type=MESH,
-            ).start()
+        zb[div(lat, 2)] = acc.astype(BF16)
+        for to in range(8):
+
+            @pl.when(div(lat, 2) != to)
+            def _(to=to):
+                pltpu.make_async_remote_copy(
+                    src_ref=zb.at[div(lat, 2)], dst_ref=zb.at[div(lat, 2)], send_sem=zb_send, recv_sem=zb_recv,
+                    device_id=(ens, 2 * to + parity, dp), device_id_type=MESH,
+                ).start()
+
         pltpu.make_async_copy(zb.at[pl.ds(0, 7)], zb.at[pl.ds(0, 7)], zb_recv).wait()
         acc = zb[0].astype(F32)
         for q in range(1, 8):
             acc = acc + zb[q].astype(F32)
         total[...] = acc.astype(BF16)
-        for _, _, device in spots:
-            pltpu.make_async_remote_copy(
-                src_ref=total, dst_ref=gw_ref.at[core, piece],
-                send_sem=ag_send, recv_sem=ag_recv, device_id=device, device_id_type=MESH,
-            ).start()
+        for l in range(2):
+            for q in range(16):
+                band_to = lat - parity + l
+
+                @pl.when(jnp.logical_or(q != y * 4 + x, band_to != lat))
+                def _(q=q, band_to=band_to):
+                    pltpu.make_async_remote_copy(
+                        src_ref=total, dst_ref=gw_ref.at[core, piece],
+                        send_sem=ag_send, recv_sem=ag_recv,
+                        device_id=(q % 8 * 2 + core, band_to, q // 8), device_id_type=MESH,
+                    ).start()
+
         pltpu.make_async_copy(total, gw_ref.at[core, piece], ag_recv).start()
 
     pltpu.make_async_copy(gw_ref.at[core], gw_ref.at[core], ag_recv).wait()

time: 48.5 us -> 47.9 us (0.988)
  Pallas kernels: 47.7 us -> 47.1 us
    pallas_call x1, Pallas kernels: 46.6 us -> 46.1 us  [local(): pl.pallas_call(kernel, out_shape=(pltpu.VMEM((CHANS * 8, 128), BF16), plt...]
where the time goes in v4:
time: 47.9 us; the launch traced here: 47.7 us
  Pallas kernels  47.1 us (98%)
  between operations  0.64 us (1%)
    pallas_call x1, Pallas kernels, local(): pl.pallas_call(kernel, out_shape=(pltpu.VMEM((CHANS * 8, 128), BF16), plt...  46.1 us
    pallas_call x1, Pallas kernels, local(): pl.pallas_call(body, out_shape=(jax.ShapeDtypeStruct((CHANS * 8, 128), BF...  1.04 us

profile of v4, /device:TPU:1, one launch (start us, length us, event | category | flops | bytes accessed | tf_op | source)
XLA Modules:
  0.0 47.7 jit_solution(15503044691106959827)
XLA Ops:
  0.6 46.1 %crps_backward.1 = (bf16[2048,128]{1,0:T(8,128)(2,1)S(1)}, bf16[2,21,32,128]{3,2,1,0:T(8,128)(2,1)S(1)}) custom-call(bf16[576,128]{1,0:T(8,128)(2,1)} %bitcast.28, f32[576,128]{1,0:T(8,128)} %bitcast.27, bf16[2048,128]{1,0:T(8,128)(2,1)} %bitcast.26, bf16[9,72,256]{2,1,0:T(8,128)(2,1)} %weight_ref.1, f32[2]{0:T(128)} %lat_ref.1, f32[72]{0:T(128)} %var_ref.1, ...), custom_call_target="tpu_custom_call" | custom-call | tf_op jit(solution)/shard_map/crps_backward/pallas_call | solution.py:408
  46.7 1.0 %write_results.1 = (bf16[2048,128]{1,0:T(8,128)(2,1)}, f32[648,256]{1,0:T(8,128)}) custom-call(bf16[2048,128]{1,0:T(8,128)(2,1)S(1)} %get-tuple-element.6.refs_0_, bf16[2,21,32,128]{3,2,1,0:T(8,128)(2,1)S(1)} %get-tuple-element.7.refs_1_), custom_call_target="tpu_custom_call" | custom-call | tf_op jit(solution)/shard_map/write_results/pallas_call | solution.py:458

commit v5 on v4

--- a/solution.py
+++ b/solution.py
@@ -105,22 +105,22 @@
 
     pl.semaphore_wait(barrier, 15 + 3)
 
-    for dx, dy in STEPS:
-        if dy > 1:
-            continue
-        for dc in range(2):
-            if dx == dy == dc == 0:
-                continue
-            to = mod(ylo + dy, 2) * 8 + mod(x + dx, 4) * 2 + mod(core + dc, 2)
-            owns, chunk = chunk_of(to)
-
-            @pl.when(owns)
-            def _(to=to, chunk=chunk):
-                pltpu.make_async_remote_copy(
-                    src_ref=members.at[pl.ds(chunk * CHUNK, CHUNK)], dst_ref=mbuf.at[ens],
-                    send_sem=exch_send, recv_sem=exch_recv,
-                    device_id=(to, lat, dp), device_id_type=MESH,
-                ).start()
+    for kind in range(4):
+
+        @pl.when(core * 2 + mod(x + ylo, 2) == kind)
+        def _(kind=kind):
+            for dx, dy in STEPS:
+                for dc in range(2):
+                    if dy > 1 or dx == dy == dc == 0:
+                        continue
+                    if (kind // 2 + dc) % 2 == 1 and (kind + dx + dy) % 2 == 0:
+                        continue
+                    to = mod(ylo + dy, 2) * 8 + mod(x + dx, 4) * 2 + (kind // 2 + dc) % 2
+                    pltpu.make_async_remote_copy(
+                        src_ref=members.at[pl.ds(chunk_of(to)[1] * CHUNK, CHUNK)], dst_ref=mbuf.at[ens],
+                        send_sem=exch_send, recv_sem=exch_recv,
+                        device_id=(to, lat, dp), device_id_type=MESH,
+                    ).start()
 
     @pl.when(owned)
     def _():
@@ -267,7 +267,7 @@
         second = jnp.logical_and(chip == 3 * third(chip), chip < 15)
         return jnp.logical_or(first, second), jnp.where(first, chip, 16 + third(chip))
 
-    spots = []
+    spots, order = [], []
     for dz in (1, 0):
         for dx, dy in STEPS:
             if dx == dy == dz == 0:
@@ -276,19 +276,32 @@
             qy = mod(y + dy, 4)
             par = parity if dz == 0 else 1 - parity
             device = (mod(qy, 2) * 8 + qx * 2 + core, lat if dz == 0 else pair, div(qy, 2))
+            order.append((dx, dy, dz))
             spots.append((qy * 4 + qx, par, device))
     place = (y * 4 + x) * 2 + parity
     sums, piece = piece_of(y * 4 + x, parity)
     piece = jnp.where(sums, piece, 0)
-    for chip, par, device in spots:
-        theirs, q = piece_of(chip, par)
-
-        @pl.when(theirs)
-        def _(q=q, device=device):
-            pltpu.make_async_remote_copy(
-                src_ref=pieces.at[pl.ds(q * PIECE, PIECE)], dst_ref=rs.at[place],
-                send_sem=rs_send, recv_sem=rs_recv, device_id=device, device_id_type=MESH,
-            ).start()
+    self_first = mod(x + y + parity, 2) == 0
+
+    def send_piece(q, device):
+        pltpu.make_async_remote_copy(
+            src_ref=pieces.at[pl.ds(q * PIECE, PIECE)], dst_ref=rs.at[place],
+            send_sem=rs_send, recv_sem=rs_recv, device_id=device, device_id_type=MESH,
+        ).start()
+
+    for odd, case in ((0, self_first), (1, jnp.logical_not(self_first))):
+
+        @pl.when(case)
+        def _(odd=odd):
+            for (chip, par, device), (dx, dy, dz) in zip(spots, order):
+                if (dx + dy + dz) % 2 == odd:
+                    send_piece(chip, device)
+                else:
+                    q = third(chip)
+
+                    @pl.when(jnp.logical_and(chip == 3 * q, chip < 15))
+                    def _(q=q, device=device):
+                        send_piece(16 + q, device)
 
     @pl.when(sums)
     def _():

time: 47.9 us -> 47.8 us (level)
  no operation moved by 1% of the time
where the time goes in v5:
time: 47.8 us; the launch traced here: 47.7 us
  Pallas kernels  47.1 us (99%)
  between operations  0.64 us (1%)
    pallas_call x1, Pallas kernels, local(): pl.pallas_call(kernel, out_shape=(pltpu.VMEM((CHANS * 8, 128), BF16), plt...  46 us
    pallas_call x1, Pallas kernels, local(): pl.pallas_call(body, out_shape=(jax.ShapeDtypeStruct((CHANS * 8, 128), BF...  1.04 us

profile of v5, /device:TPU:1, one launch (start us, length us, event | category | flops | bytes accessed | tf_op | source)
XLA Modules:
  0.0 47.7 jit_solution(4421349872899222247)
XLA Ops:
  0.6 46.0 %crps_backward.1 = (bf16[2048,128]{1,0:T(8,128)(2,1)S(1)}, bf16[2,21,32,128]{3,2,1,0:T(8,128)(2,1)S(1)}) custom-call(bf16[576,128]{1,0:T(8,128)(2,1)} %bitcast.28, f32[576,128]{1,0:T(8,128)} %bitcast.27, bf16[2048,128]{1,0:T(8,128)(2,1)} %bitcast.26, bf16[9,72,256]{2,1,0:T(8,128)(2,1)} %weight_ref.1, f32[2]{0:T(128)} %lat_ref.1, f32[72]{0:T(128)} %var_ref.1, ...), custom_call_target="tpu_custom_call" | custom-call | tf_op jit(solution)/shard_map/crps_backward/pallas_call | solution.py:421
  46.7 1.0 %write_results.1 = (bf16[2048,128]{1,0:T(8,128)(2,1)}, f32[648,256]{1,0:T(8,128)}) custom-call(bf16[2048,128]{1,0:T(8,128)(2,1)S(1)} %get-tuple-element.6.refs_0_, bf16[2,21,32,128]{3,2,1,0:T(8,128)(2,1)S(1)} %get-tuple-element.7.refs_1_), custom_call_target="tpu_custom_call" | custom-call | tf_op jit(solution)/shard_map/write_results/pallas_call | solution.py:471
